TPU v7x, 32 devices: a whole 2x2x4 slice. The times are simulated.
32 devices in a mesh: groups: 2 (over y), blk: 16 (over z, x, core).
Axes of the slice: x: 2, y: 2, z: 4, core: 2. Of those that a mesh axis runs over, the one named last changes fastest.
Arguments:
- train_rows: bfloat16 [8192, 8192], P(('groups', 'blk')), parts along dimension 0, may hold values from -6 to 6
- pair_ids: int32 [8192], P(('groups', 'blk')), parts along dimension 0, may hold values from 0 to 127, as said below
- pair_owner: int32 [4096, 1], P(('groups', 'blk')), parts along dimension 0, may hold values from 0 to 15; in each aligned block of 128 rows (0 to 127, 128 to 255, ...) at most 16 rows name the same one
- second_moment: float32 [8192], replicated, may hold values from 0.0001 to 0.1
- val_rows: bfloat16 [128, 8192], P('blk'), may hold values from -6 to 6
Outputs:
- influence: bfloat16 [16384, 128], P(('groups', 'blk')), parts along dimension 0
- order_gap: bfloat16 [8192, 128], P(('groups', 'blk')), parts along dimension 0
There are 2 independent parts, one for each index of `groups`. A program takes and returns all parts, laid end to end along the dimension named above; an argument that names none is the same for every part. Nothing has to cross between parts.
Inputs may be any that keep to these rules, and one draw needn't show every extreme that they name: `pair_ids`: within each aligned block of 256 rows every pair number appears exactly twice; the first appearance is the forward order, the second the swapped one. `pair_owner`: within the 128 pairs of one device no owner is named more than 16 times.
All inputs are finite; a program needn't handle non-finite values.
Results may differ from a plain program's by a relative error of at most 0.0065.
Values may be sent and summed in bfloat16 or wider, within the bound.
A program may use at most 128 MiB of HBM per device.

v0:
```python
import math

import jax
import jax.numpy as jnp
from jax import lax
from jax.sharding import PartitionSpec as P

epsilon = 1e-05


def unit_rows(rows):
    wide = rows.astype(jnp.float32)
    return (wide * lax.rsqrt(jnp.mean(wide * wide, axis=1, keepdims=True) + epsilon)).astype(
        jnp.bfloat16
    )


def against_val(unit_left, val_unit):
    features = unit_left.shape[1]
    contract = (((1,), (1,)), ((), ()))
    gathered = lax.all_gather(val_unit, "blk", axis=0, tiled=True)
    return lax.dot_general(
        unit_left, gathered, contract, preferred_element_type=jnp.float32
    ) / math.sqrt(features)


def on_device(train_rows, pair_ids, pair_owner, second_moment, val_rows):
    members = lax.axis_size("blk")
    row_total = train_rows.shape[0]
    pair_total = row_total // 2
    capacity = max(2, 2 * pair_total // members)
    features = train_rows.shape[1]
    owners = pair_owner[:, 0]
    owner_hot = (owners[:, None] == jnp.arange(members, dtype=jnp.int32)[None, :]).astype(jnp.int32)
    position = jnp.sum((jnp.cumsum(owner_hot, axis=0) - owner_hot) * owner_hot, axis=1)
    pair_hot = (pair_ids[:, None] == jnp.arange(pair_total, dtype=jnp.int32)[None, :]).astype(
        jnp.int32
    )
    second = jnp.sum((jnp.cumsum(pair_hot, axis=0) - pair_hot) * pair_hot, axis=1)
    target = owners[pair_ids] * (2 * capacity) + 2 * position[pair_ids] + second
    precondition = 1.0 / (jnp.sqrt(second_moment) + 1e-08)
    scaled = (train_rows.astype(jnp.float32) * precondition[None, :]).astype(jnp.bfloat16)
    val_unit = unit_rows(val_rows)
    slot_count = members * 2 * capacity
    outgoing = jnp.zeros((slot_count, features), jnp.bfloat16).at[target].set(scaled)
    outgoing = outgoing.reshape(members, 2 * capacity, features)
    arrived = lax.all_to_all(outgoing, "blk", split_axis=0, concat_axis=0, tiled=True).reshape(
        slot_count, features
    )
    scores = against_val(unit_rows(arrived), val_unit)
    paired = scores.reshape(-1, 2, scores.shape[1])
    return (scores.astype(jnp.bfloat16), (paired[:, 0] - paired[:, 1]).astype(jnp.bfloat16))


def solution(mesh):
    return jax.shard_map(
        on_device,
        mesh=mesh,
        in_specs=(
            P(("groups", "blk"), None),
            P(("groups", "blk")),
            P(("groups", "blk"), None),
            P(),
            P("blk", None),
        ),
        out_specs=(P(("groups", "blk"), None), P(("groups", "blk"), None)),
        check_vma=False,
    )
```

profile of v0, /device:TPU:11, one launch (start us, length us, event | category | flops | bytes accessed | tf_op | source)
XLA Modules:
  0.0 259.7 jit_solution(12799240794216690755)
XLA Ops:
  7.2 0.7 fusion.12
  7.9 0.2 reduce_window_sum.26
  8.1 0.8 select_reduce_fusion
  8.9 0.7 compare_select_fusion.1
  9.6 1.9 gather_fusion
  11.5 1.9 gather_fusion.1
  13.4 0.8 copy.9
  14.2 0.2 fusion.6
  14.5 0.9 fusion.8
  15.4 0.8 add_divide_fusion
  16.1 12.4 %scatter_custom_fusion = bf16[512,8192]{1,0:T(8,128)(2,1)} fusion(s32[256]{0:T(256)S(1)} %bitcast.41, bf16[256,8192]{1,0:T(8,128)(2,1)} %param.5, f32[8192]{0:T(1024)S(1)} %add_divide_fusion, bf16[]{:T(256)} %constant.12.clone.1), kind=kCustom, calls=%fused_computation.7 | custom fusion | flops 6291456 | bytes 12615682 | tf_op jit(solution)/shard_map/scatter | solution.py:45
  28.5 0.0 copy-start
  28.6 6.7 %all-to-all-start = ((bf16[16,32,8192]{2,1,0:T(8,128)(2,1)}), bf16[16,32,8192]{2,1,0:T(8,128)(2,1)}, u32[]{:S(2)}, u32[]{:S(2)}) async-start(bf16[16,32,8192]{2,1,0:T(8,128)(2,1)} %bitcast.32), calls=%async_computation | async-start | bytes 16777216 | tf_op jit(solution)/shard_map/all_to_all | solution.py:47
  35.2 0.2 all-gather.2.cloned.1.call-start
  35.5 0.0 copy-done
  35.5 0.2 fusion.4
  35.7 0.8 fusion.5
  36.4 0.0 all-gather.2.cloned.1.call-update
  36.4 193.8 %all-to-all-done = bf16[16,32,8192]{2,1,0:T(8,128)(2,1)} async-done(((bf16[16,32,8192]{2,1,0:T(8,128)(2,1)}), bf16[16,32,8192]{2,1,0:T(8,128)(2,1)}, u32[]{:S(2)}, u32[]{:S(2)}) %all-to-all-start) | async-done | bytes 8388640 | tf_op jit(solution)/shard_map/all_to_all | solution.py:47
  230.3 5.1 %multiply_reduce_fusion = f32[16,32]{1,0:T(8,128)S(1)} fusion(bf16[16,32,8192]{2,1,0:T(8,128)(2,1)} %all-to-all-done), kind=kLoop, calls=%fused_computation.5 | loop fusion | flops 12582400 | bytes 8390656 | tf_op jit(solution)/shard_map/reduce_sum | solution.py:13
  235.4 0.1 rsqrt.20
  235.5 9.6 %fusion = bf16[512,8192]{1,0:T(8,128)(2,1)} fusion(f32[512]{0:T(512)S(1)} %rsqrt.20, bf16[16,32,8192]{2,1,0:T(8,128)(2,1)} %all-to-all-done), kind=kLoop, calls=%fused_computation.4 | loop fusion | flops 12582912 | bytes 16779264 | tf_op jit(solution)/shard_map/convert_element_type | solution.py:13
  245.0 0.0 all-gather.2.cloned.1.call-done
  245.0 7.0 %fusion.14 = (bf16[512,128]{1,0:T(8,128)(2,1)}, f32[512,128]{1,0:T(8,128)S(1)}) fusion(bf16[512,8192]{1,0:T(8,128)(2,1)} %fusion, bf16[128,8192]{1,0:T(8,128)(2,1)} %all-gather.2.cloned.1.call-done), kind=kOutput, calls=%fused_computation.38 | convolution fusion | flops 1073872896 | bytes 10878976 | tf_op jit(solution)/shard_map/dot_general | solution.py:22
  252.0 0.2 fusion.13
  252.2 0.6 fusion.10
  (11 shorter events, 0.1 us)
Async XLA Ops:
  28.5 6.9 %copy-start = (bf16[8,8192]{1,0:T(8,128)(2,1)S(1)}, bf16[8,8192]{1,0:T(8,128)(2,1)}, u32[]{:S(2)}) copy-start(bf16[8,8192]{1,0:T(8,128)(2,1)} %param.9) | copy-start | bytes 393220
  28.6 201.7 %all-to-all-start = ((bf16[16,32,8192]{2,1,0:T(8,128)(2,1)}), bf16[16,32,8192]{2,1,0:T(8,128)(2,1)}, u32[]{:S(2)}, u32[]{:S(2)}) async-start(bf16[16,32,8192]{2,1,0:T(8,128)(2,1)} %bitcast.32), calls=%async_computation | async-start | bytes 16777216 | tf_op jit(solution)/shard_map/all_to_all | solution.py:47
  35.2 209.8 %all-gather.2.cloned.1.call-start = ((), (), s32[]{:S(2)}) async-start(), calls=%async_computation.1 | async-start | bytes 2228224 | tf_op jit(solution)/shard_map/all_gather | solution.py:21
Sparse Core Ops, SparseCore 0:
  38.8 143.4 all-gather.1
where the time goes:
time: 260 us
  waiting for transfers between devices  194 us (75%)
  other arithmetic  33 us (13%)
  between operations  14.1 us (5%)
  matrix products  6.97 us (3%)
  starting transfers between devices  6.9 us (3%)
  local copies, waits for them, and re-layouts  4.86 us (2%)
    all_to_all x1, waiting for transfers between devices, on_device(): lax.all_to_all(outgoing, 'blk', split_axis=0, concat_axis=0, tiled=True)  194 us
    scatter x1, other arithmetic, on_device(): jnp.zeros((slot_count, features), jnp.bfloat16).at[target].set(scaled)  12.4 us
    convert_element_type x2, other arithmetic, unit_rows(): (wide * lax.rsqrt(jnp.mean(wide * wide, axis=1, keepdims=True) + epsilon)...  10.3 us
    dot_general x1, matrix products, against_val(): lax.dot_general(unit_left, gathered, contract, preferred_element_type=jnp...  6.97 us
    all_to_all x1, starting transfers between devices, on_device(): lax.all_to_all(outgoing, 'blk', split_axis=0, concat_axis=0, tiled=True)  6.69 us
    reduce_sum x2, other arithmetic, unit_rows(): jnp.mean(wide * wide, axis=1, keepdims=True) + epsilon  5.28 us
  transfers between devices with their start and end apart: 2, of which 1 were waited for; matrix products, arithmetic and copies ran while one was open for 6% of the time, Pallas kernels for 0%

commit v1 on v0

v1 whole, which is shorter than its diff:
```python
import math

import jax
import jax.numpy as jnp
from jax import lax
from jax.sharding import PartitionSpec as P

epsilon = 1e-05


def unit_rows(rows):
    wide = rows.astype(jnp.float32)
    return (wide * lax.rsqrt(jnp.mean(wide * wide, axis=1, keepdims=True) + epsilon)).astype(
        jnp.bfloat16
    )


def on_device(train_rows, pair_ids, pair_owner, second_moment, val_rows):
    members = lax.axis_size("blk")
    row_total, features = train_rows.shape
    pair_total = row_total // 2
    capacity = max(2, 2 * pair_total // members)
    gathered = lax.all_gather(unit_rows(val_rows), "blk", axis=0, tiled=True)
    vals = gathered.shape[0]
    owner_hot = (pair_owner == jnp.arange(members, dtype=jnp.int32)[None, :]).astype(jnp.float32)
    before = jnp.tri(pair_total, k=-1, dtype=jnp.float32)
    position = jnp.sum(jnp.dot(before, owner_hot) * owner_hot, axis=1, keepdims=True)
    place = pair_owner.astype(jnp.float32) * (2 * capacity) + 2 * position
    pair_hot = (jnp.arange(pair_total, dtype=jnp.int32)[:, None] == pair_ids[None, :]).astype(jnp.float32)
    earlier = jnp.dot(pair_hot, jnp.tri(row_total, k=-1, dtype=jnp.float32).T)
    target = jnp.sum(pair_hot * (place + earlier), axis=0).astype(jnp.int32)
    slot_count = members * 2 * capacity
    hot = (jnp.arange(slot_count, dtype=jnp.int32)[:, None] == target[None, :]).astype(jnp.bfloat16)
    precondition = 1.0 / (jnp.sqrt(second_moment) + 1e-08)
    scaled = (train_rows.astype(jnp.float32) * precondition[None, :]).astype(jnp.bfloat16)
    live = lax.dot_general(
        unit_rows(scaled), gathered, (((1,), (1,)), ((), ())), preferred_element_type=jnp.float32
    ) / math.sqrt(features)
    high = live.astype(jnp.bfloat16)
    low = (live - high.astype(jnp.float32)).astype(jnp.bfloat16)
    influence = jnp.dot(hot, high, preferred_element_type=jnp.float32)
    rest = jnp.dot(hot, low, preferred_element_type=jnp.float32)
    paired = (influence + rest).reshape(-1, 2, vals)
    gap = paired[:, 0] - paired[:, 1]
    sent = jnp.concatenate(
        [
            influence.astype(jnp.bfloat16).reshape(members, 2 * capacity, vals),
            gap.astype(jnp.bfloat16).reshape(members, capacity, vals),
        ],
        axis=1,
    )
    arrived = lax.all_to_all(sent, "blk", split_axis=0, concat_axis=0, tiled=True)
    return (
        arrived[:, : 2 * capacity].reshape(slot_count, vals),
        arrived[:, 2 * capacity :].reshape(slot_count // 2, vals),
    )


def solution(mesh):
    return jax.shard_map(
        on_device,
        mesh=mesh,
        in_specs=(
            P(("groups", "blk"), None),
            P(("groups", "blk")),
            P(("groups", "blk"), None),
            P(),
            P("blk", None),
        ),
        out_specs=(P(("groups", "blk"), None), P(("groups", "blk"), None)),
        check_vma=False,
    )
```

time: 260 us -> 80.6 us (0.31)
  the two profiles are of different devices: /device:TPU:11 before, /device:TPU:0 now
where the time goes in v1:
time: 80.6 us; the launch traced here: 80.2 us
  waiting for transfers between devices  38 us (47%)
  between operations  14.1 us (17%)
  blocking collectives  12.3 us (15%)
  other arithmetic  7.68 us (10%)
  matrix products  6.68 us (8%)
  local copies, waits for them, and re-layouts  1.5 us (2%)
    all_gather x1, waiting for transfers between devices, on_device(): gathered = lax.all_gather(unit_rows(val_rows), 'blk', axis=0, tiled=True)  38 us
    all_to_all x1, blocking collectives, on_device(): lax.all_to_all(sent, 'blk', split_axis=0, concat_axis=0, tiled=True)  12.3 us
    reduce_sum x2, other arithmetic, unit_rows(): jnp.mean(wide * wide, axis=1, keepdims=True) + epsilon  4.51 us
    dot_general x1, matrix products, on_device(): lax.dot_general(unit_rows(scaled), gathered, (((1,), (1,)), ((), ())), pr...  4.2 us
    convert_element_type x1, other arithmetic, unit_rows(): (wide * lax.rsqrt(jnp.mean(wide * wide, axis=1, keepdims=True) + epsilon)...  1.65 us
  transfers between devices with their start and end apart: 1, of which 1 were waited for; matrix products, arithmetic and copies ran while one was open for 9% of the time, Pallas kernels for 0%

profile of v1, /device:TPU:0, one launch (start us, length us, event | category | flops | bytes accessed | tf_op | source)
XLA Modules:
  0.0 80.2 jit_solution(7057597600215888749)
XLA Ops:
  7.2 0.0 all-gather.2.cloned.1.call-start
  7.2 1.1 %fusion.12 = f32[8]{0:T(128)S(1)} fusion(bf16[8,8192]{1,0:T(8,128)(2,1)} %param.9), kind=kLoop, calls=%fused_computation.18 | loop fusion | flops 196600 | bytes 131104 | tf_op jit(solution)/shard_map/reduce_sum | solution.py:13
  8.3 1.7 %fusion.13 = bf16[8,8192]{1,0:T(8,128)(2,1)} fusion(bf16[8,8192]{1,0:T(8,128)(2,1)} %param.9, f32[8]{0:T(128)S(1)} %add_rsqrt_fusion.1), kind=kLoop, calls=%fused_computation.19 | loop fusion | flops 196608 | bytes 262176 | tf_op jit(solution)/shard_map/convert_element_type | solution.py:13
  10.0 0.0 all-gather.2.cloned.1.call-update
  10.0 0.9 %fusion.10 = f32[128]{0:T(128)S(1)} fusion(s32[128]{0:T(128)S(1)} %iota_add_fusion.1, s32[128]{0:T(128)} %bitcast.22), kind=kOutput, calls=%fused_computation.13 | convolution fusion | flops 548736 | bytes 1536 | tf_op jit(solution)/shard_map/dot_general | solution.py:27
  10.9 0.7 fusion.22
  11.6 1.1 %fusion.9 = f32[256]{0:T(256)S(1)} fusion(s32[256]{0:T(256)S(1)} %iota_add_fusion, f32[128]{0:T(128)S(1)} %fusion.22, s32[256]{0:T(256)} %param.6), kind=kOutput, calls=%fused_computation.11 | convolution fusion | flops 17006336 | bytes 3584 | tf_op jit(solution)/shard_map/dot_general | solution.py:30
  12.7 0.8 add_divide_fusion
  13.5 3.4 %fusion = f32[256]{0:T(256)S(1)} fusion(f32[8192]{0:T(1024)S(1)} %add_divide_fusion, bf16[256,8192]{1,0:T(8,128)(2,1)} %param.5), kind=kLoop, calls=%fused_computation.2 | loop fusion | flops 12582656 | bytes 4228096 | tf_op jit(solution)/shard_map/reduce_sum | solution.py:13
  16.9 38.0 %all-gather.2.cloned.1.call-done = bf16[128,8192]{1,0:T(8,128)(2,1)} async-done(((bf16[8,8192]{1,0:T(8,128)(2,1)}), bf16[128,8192]{1,0:T(8,128)(2,1)}) %all-gather.2.cloned.1.call-update) | async-done | bytes 2097168 | tf_op jit(solution)/shard_map/all_gather | solution.py:23
  54.9 4.2 %fusion.6 = f32[256,128]{1,0:T(8,128)S(1)} fusion(bf16[128,8192]{1,0:T(8,128)(2,1)} %all-gather.2.cloned.1.call-done, f32[256]{0:T(256)S(1)} %add_rsqrt_fusion, f32[8192]{0:T(1024)S(1)} %add_divide_fusion, bf16[256,8192]{1,0:T(8,128)(2,1)} %param.5), kind=kOutput, calls=%fused_computation.10 | convolution fusion | flops 549486592 | bytes 6456320 | tf_op jit(solution)/shard_map/dot_general | solution.py:36
  59.1 0.2 fusion.24
  59.3 0.2 convolution_add_fusion
  59.6 0.2 fusion.23
  59.8 12.3 %all_to_all.5 = bf16[16,48,128]{2,1,0:T(8,128)(2,1)S(1)} all-to-all(bf16[16,48,128]{2,1,0:T(8,128)(2,1)S(1)} %pad_maximum_fusion), channel_id=1, replica_groups=mesh['groups'=2,'blk'=16] {'blk'}, dimensions={0} | all-to-all | bytes 393216 | tf_op jit(solution)/shard_map/all_to_all | solution.py:52
  72.1 0.7 slice.18
  72.8 0.6 slice.19
  (7 shorter events, 0.1 us)
Async XLA Ops:
  7.2 47.7 %all-gather.2.cloned.1.call-start = ((), (), s32[]{:S(2)}) async-start(), calls=%async_computation.1 | async-start | bytes 2228224 | tf_op jit(solution)/shard_map/all_gather | solution.py:23
Sparse Core Ops, SparseCore 0:
  10.7 44.1 all-gather.1

commit v2 on v1

--- a/solution.py
+++ b/solution.py
@@ -1,8 +1,11 @@
+import functools
 import math
 
 import jax
 import jax.numpy as jnp
 from jax import lax
+from jax.experimental import pallas as pl
+from jax.experimental.pallas import tpu as pltpu
 from jax.sharding import PartitionSpec as P
 
 epsilon = 1e-05
@@ -15,7 +18,7 @@
     )
 
 
-def on_device(train_rows, pair_ids, pair_owner, second_moment, val_rows):
+def plain(train_rows, pair_ids, pair_owner, second_moment, val_rows):
     members = lax.axis_size("blk")
     row_total, features = train_rows.shape
     pair_total = row_total // 2
@@ -56,6 +59,274 @@
     )
 
 
+MESH = pl.DeviceIdType.MESH
+CHUNKS = 4
+COLS = 2
+STRIP = 16
+
+
+def hot_places(ids, owners, capacity):
+    pairs, rows = owners.shape[0], ids.shape[1]
+    iota = lax.broadcasted_iota
+    owner_hot = (iota(jnp.int32, (pairs, 128), 1) == owners).astype(jnp.float32)
+    before = (iota(jnp.int32, (pairs, pairs), 1) < iota(jnp.int32, (pairs, pairs), 0)).astype(jnp.float32)
+    counts = jnp.dot(before.astype(jnp.bfloat16), owner_hot.astype(jnp.bfloat16), preferred_element_type=jnp.float32)
+    position = jnp.sum(counts * owner_hot, axis=1, keepdims=True)
+    place = owners.astype(jnp.float32) * capacity + position
+    pair_hot = (iota(jnp.int32, (pairs, rows), 0) == ids).astype(jnp.float32)
+    after = (iota(jnp.int32, (rows, rows), 0) < iota(jnp.int32, (rows, rows), 1)).astype(jnp.float32)
+    earlier = jnp.dot(pair_hot.astype(jnp.bfloat16), after.astype(jnp.bfloat16), preferred_element_type=jnp.float32)
+    slot = jnp.sum(pair_hot * place, axis=0, keepdims=True)
+    second = jnp.sum(pair_hot * earlier, axis=0, keepdims=True)
+    return slot, second
+
+
+def kernel(
+    members, capacity,
+    train_ref, ids_ref, owner_ref, moment_ref, val_ref,
+    influence_ref, gap_ref,
+    rows, pre, squares, held, hot, signed, outbox, inbox,
+    row_sem, z_send, x_send, y_send, c_send, held_sem, out_send, out_recv,
+):
+    depth = members // (2 * COLS)
+    total, features = train_ref.shape
+    vals = val_ref.shape[0]
+    wide = features // CHUNKS
+    half = wide // 2
+    slots = members * capacity
+    me = lax.axis_index("blk")
+    group = lax.axis_index("groups")
+    core = lax.rem(me, 2)
+    col = lax.rem(me // 2, COLS)
+    layer = me // (2 * COLS)
+
+    def at(dz, dx, dc=0):
+        z = lax.rem(layer + dz, depth)
+        x = lax.rem(col + dx, COLS)
+        return (z * COLS + x) * 2 + lax.rem(core + dc, 2)
+
+    here = (group, me)
+    aside = (group, at(0, 1))
+    across = (1 - group, me)
+    sibling = (group, at(0, 0, 1))
+
+    fetches = []
+    for k in range(CHUNKS):
+        lanes = pl.ds(k * wide, wide)
+        copy = pltpu.make_async_copy(train_ref.at[:, lanes], rows.at[:, lanes], row_sem.at[k])
+        copy.start()
+        fetches.append(copy)
+
+    barrier = pltpu.get_barrier_semaphore()
+    for step in range(1, members):
+        pl.semaphore_signal(barrier, 1, device_id=(group, lax.rem(me + step, members)), device_id_type=MESH)
+    pl.semaphore_signal(barrier, 1, device_id=across, device_id_type=MESH)
+
+    val = val_ref[...].astype(jnp.float32)
+    unit = val * lax.rsqrt(jnp.mean(val * val, axis=1, keepdims=True) + epsilon)
+    for k in range(CHUNKS):
+        both = [unit[:, k * wide + h * half : k * wide + (h + 1) * half] for h in range(2)]
+        held[k, pl.ds(me, 1)] = jnp.concatenate(both, axis=0).astype(jnp.bfloat16)[None]
+    pl.semaphore_wait(barrier, members)
+
+    sends = []
+
+    def send(k, m, sem, to):
+        copy = pltpu.make_async_remote_copy(
+            src_ref=held.at[k, m], dst_ref=held.at[k, m], send_sem=sem, recv_sem=held_sem.at[k, m],
+            device_id=to, device_id_type=MESH,
+        )
+        copy.start()
+        sends.append(copy)
+
+    def arrived(k, m):
+        pltpu.make_async_remote_copy(
+            src_ref=held.at[k, m], dst_ref=held.at[k, m], send_sem=out_send.at[0], recv_sem=held_sem.at[k, m],
+            device_id=sibling, device_id_type=MESH,
+        ).wait_recv()
+
+    def to_core(k, dz, dx):
+        send(k, at(dz, dx), c_send.at[k, dx * depth + dz], sibling)
+
+    def to_side(k, dz):
+        send(k, at(dz, 0), x_send.at[k, dz], aside)
+
+    def to_group(k, dz, dx):
+        send(k, at(dz, dx), y_send.at[k, dx * depth + dz], across)
+
+    steps = range(1, depth)
+    own = [2 * j + group for j in range(CHUNKS // 2)]
+    other = [2 * j + 1 - group for j in range(CHUNKS // 2)]
+
+    for j in range(CHUNKS // 2):
+        for dz in steps:
+            send(own[j], me, z_send.at[j, dz - 1], (group, at(dz, 0)))
+        to_side(own[j], 0)
+        if j % 2:
+            to_side(other[j], 0)
+        to_core(own[j], 0, 0)
+        to_core(other[j], 0, 0)
+
+    def from_z(j):
+        for dz in steps:
+            arrived(own[j], at(dz, 0))
+            to_side(own[j], dz)
+            to_group(own[j], dz, 0)
+            to_core(own[j], dz, 0)
+
+    def side_own(j):
+        for dz in range(depth):
+            arrived(own[j], at(dz, 1))
+            if j % 2 == 0:
+                to_group(own[j], dz, 1)
+            to_core(own[j], dz, 1)
+
+    def group_near(j):
+        for dz in steps:
+            arrived(other[j], at(dz, 0))
+            if j % 2:
+                to_side(other[j], dz)
+            to_core(other[j], dz, 0)
+
+    def far(j):
+        for dz in range(depth):
+            arrived(other[j], at(dz, 1))
+            to_core(other[j], dz, 1)
+
+    def from_core(j):
+        for k in (own[j], other[j]):
+            for dz in range(depth):
+                for dx in range(COLS):
+                    arrived(k, at(dz, dx, 1))
+
+    def scale(k):
+        fetches[k].wait()
+        lanes = pl.ds(k * wide, wide)
+
+        def strip(i, _):
+            band = pl.ds(pl.multiple_of(i * STRIP, STRIP), STRIP)
+            scaled = (rows[band, lanes].astype(jnp.float32) * pre[:, lanes]).astype(jnp.bfloat16)
+            rows[band, lanes] = scaled
+            scaled = scaled.astype(jnp.float32)
+            found = jnp.sum(scaled * scaled, axis=1, keepdims=True)
+            squares[band, :] = found if k == 0 else squares[band, :] + found
+            return 0
+
+        lax.fori_loop(0, total // STRIP, strip, 0)
+
+    def product(k):
+        block = held[k].astype(jnp.float32)
+        result = None
+        for h in range(2):
+            piece = block[:, h * vals : (h + 1) * vals].reshape(members * vals, half).astype(jnp.bfloat16)
+            left = rows[:, pl.ds(k * wide + h * half, half)]
+            term = lax.dot_general(left, piece, (((1,), (1,)), ((), ())), preferred_element_type=jnp.float32)
+            result = term if result is None else result + term
+        return result
+
+    pre[...] = 1.0 / (jnp.sqrt(moment_ref[...]) + 1e-08)
+    scale(0)
+    from_z(0)
+    scale(1)
+    side_own(0)
+    from_z(1)
+    scale(2)
+    group_near(1)
+    group_near(0)
+    scale(3)
+    side_own(1)
+    far(0)
+    slot, second = hot_places(ids_ref[...], owner_ref[...], capacity)
+    place = lax.broadcasted_iota(jnp.int32, (2 * slots, total), 0).astype(jnp.float32)
+    hot[...] = (place == 2 * slot + second).astype(jnp.float32).astype(jnp.bfloat16)
+    place = lax.broadcasted_iota(jnp.int32, (slots, total), 0).astype(jnp.float32)
+    signed[...] = jnp.where(place == slot, 1 - 2 * second, 0.0).astype(jnp.bfloat16)
+    from_core(0)
+    live = product(0) + product(1)
+    far(1)
+    from_core(1)
+    live = live + product(2) + product(3)
+    live = live * (lax.rsqrt(squares[...] / features + epsilon) / math.sqrt(features))
+
+    high = live.astype(jnp.bfloat16)
+    low = (live - high.astype(jnp.float32)).astype(jnp.bfloat16)
+    influence = jnp.dot(hot[...], high, preferred_element_type=jnp.float32)
+    gap = jnp.dot(signed[...], high, preferred_element_type=jnp.float32)
+    gap = gap + jnp.dot(signed[...], low, preferred_element_type=jnp.float32)
+    outbox[:, : 2 * capacity] = influence.astype(jnp.bfloat16).reshape(members, 2 * capacity, -1)
+    outbox[:, 2 * capacity :] = gap.astype(jnp.bfloat16).reshape(members, capacity, -1)
+
+    for step in range(1, members):
+        to = lax.rem(me + step, members)
+        copy = pltpu.make_async_remote_copy(
+            src_ref=outbox.at[to], dst_ref=inbox.at[me], send_sem=out_send.at[step], recv_sem=out_recv.at[me],
+            device_id=(group, to), device_id_type=MESH,
+        )
+        copy.start()
+        sends.append(copy)
+
+    def place_block(m, ref):
+        influence_ref[pl.ds(pl.multiple_of(m * 2 * capacity, 2 * capacity), 2 * capacity), :] = ref[m, : 2 * capacity]
+        gap_ref[pl.ds(pl.multiple_of(m * capacity, capacity), capacity), :] = ref[m, 2 * capacity :]
+
+    place_block(me, outbox)
+    for step in range(1, members):
+        m = lax.rem(me + members - step, members)
+        pltpu.make_async_remote_copy(
+            src_ref=outbox.at[m], dst_ref=inbox.at[m], send_sem=out_send.at[0], recv_sem=out_recv.at[m],
+            device_id=sibling, device_id_type=MESH,
+        ).wait_recv()
+        place_block(m, inbox)
+    for copy in sends:
+        copy.wait_send()
+
+
+def on_device(train_rows, pair_ids, pair_owner, second_moment, val_rows):
+    members = lax.axis_size("blk")
+    total, features = train_rows.shape
+    capacity = max(2, total // members)
+    vals = val_rows.shape[0]
+    if capacity % 16 or members % (2 * COLS) or lax.axis_size("groups") != 2:
+        return plain(train_rows, pair_ids, pair_owner, second_moment, val_rows)
+    slots, width, wide = members * capacity, members * vals, features // CHUNKS
+    depth = members // (2 * COLS)
+    vmem = pl.BlockSpec(memory_space=pltpu.VMEM)
+    dma = pltpu.SemaphoreType.DMA
+    return pl.pallas_call(
+        functools.partial(kernel, members, capacity),
+        out_shape=(
+            jax.ShapeDtypeStruct((2 * slots, width), jnp.bfloat16),
+            jax.ShapeDtypeStruct((slots, width), jnp.bfloat16),
+        ),
+        in_specs=[pl.BlockSpec(memory_space=pl.ANY), vmem, vmem, vmem, vmem],
+        out_specs=(vmem, vmem),
+        scratch_shapes=[
+            pltpu.VMEM((total, features), jnp.bfloat16),
+            pltpu.VMEM((1, features), jnp.float32),
+            pltpu.VMEM((total, 1), jnp.float32),
+            pltpu.VMEM((CHUNKS, members, 2 * vals, wide // 2), jnp.bfloat16),
+            pltpu.VMEM((2 * slots, total), jnp.bfloat16),
+            pltpu.VMEM((slots, total), jnp.bfloat16),
+            pltpu.VMEM((members, 3 * capacity, width), jnp.bfloat16),
+            pltpu.VMEM((members, 3 * capacity, width), jnp.bfloat16),
+            dma((CHUNKS,)),
+            dma((CHUNKS // 2, depth)),
+            dma((CHUNKS, depth)),
+            dma((CHUNKS, COLS * depth)),
+            dma((CHUNKS, COLS * depth)),
+            dma((CHUNKS, members)),
+            dma((members,)),
+            dma((members,)),
+        ],
+        compiler_params=pltpu.CompilerParams(
+            collective_id=0, has_side_effects=True, vmem_limit_bytes=48 * 2**20
+        ),
+        cost_estimate=pl.CostEstimate(
+            flops=2 * total * features * width, bytes_accessed=2 * total * features, transcendentals=0
+        ),
+    )(train_rows, pair_ids.reshape(1, total), pair_owner, second_moment.reshape(1, features), val_rows)
+
+
 def solution(mesh):
     return jax.shard_map(
         on_device,

time: 80.6 us -> 40.5 us (0.50)
  waiting for transfers between devices: 38 us -> 0 us
  Pallas kernels: 0 us -> 33 us
  between operations: 14.1 us -> 0.65 us
  blocking collectives: 12.3 us -> 0 us
  other arithmetic: 7.68 us -> 0 us
  matrix products: 6.68 us -> 0 us
  local copies, waits for them, and re-layouts: 1.5 us -> 6.57 us
    all_gather x1 -> x0, waiting for transfers between devices: 38 us -> none  [on_device(): gathered = lax.all_gather(unit_rows(val_rows), 'blk', axis=0, tiled=True)]
    pallas_call x0 -> x1, Pallas kernels: none -> 33 us  [on_device(): pl.pallas_call(functools.partial(kernel, members, capacity), out_shape=(j...]
    all_to_all x1 -> x0, blocking collectives: 12.3 us -> none  [on_device(): lax.all_to_all(sent, 'blk', split_axis=0, concat_axis=0, tiled=True)]
    dot_general x5 -> x0, matrix products: 6.68 us -> none  [the longest x1 4.2 us: on_device(): lax.dot_general(unit_rows(scaled), gathered, (((1,), (1,)), ((), ())), pr...]
    unnamed x0 -> x11, local copies, waits for them, and re-layouts: none -> 6.57 us
    reduce_sum x2 -> x0, other arithmetic: 4.51 us -> none  [unit_rows(): jnp.mean(wide * wide, axis=1, keepdims=True) + epsilon]
    convert_element_type x3 -> x0, other arithmetic: 1.67 us -> none  [the longest x1 1.65 us: unit_rows(): (wide * lax.rsqrt(jnp.mean(wide * wide, axis=1, keepdims=True) + epsilon)...]
    slice x3 -> x0, local copies, waits for them, and re-layouts: 1.5 us -> none  [the longest x1 0.66 us: on_device(): arrived[:, :2 * capacity].reshape(slot_count, vals)]
  transfers between devices with their start and end apart: 1 -> 0, of which waited for: 1 -> 0; matrix products, arithmetic and copies ran while one was open for 9% -> 0% of each run, Pallas kernels for 0% -> 0%
where the time goes in v2:
time: 40.5 us; the launch traced here: 40.2 us
  Pallas kernels  33 us (81%)
  local copies, waits for them, and re-layouts  6.57 us (16%)
  between operations  0.65 us (2%)
    pallas_call x1, Pallas kernels, on_device(): pl.pallas_call(functools.partial(kernel, members, capacity), out_shape=(j...  33 us
    unnamed x11, local copies, waits for them, and re-layouts  6.57 us

profile of v2, /device:TPU:0, one launch (start us, length us, event | category | flops | bytes accessed | tf_op | source)
XLA Modules:
  0.0 40.2 jit_solution(4722207896094850259)
XLA Ops:
  0.6 0.8 %copy.7.owner_ref = s32[128,1]{1,0:T(8,128)S(1)} copy(s32[128,1]{0,1:T(1,128)} %param.7) | data formatting | bytes 1024 | tf_op args[2]
  1.4 0.0 copy-start
  1.4 2.2 %copy-done = bf16[256,8192]{1,0:T(8,128)(2,1)S(1)} copy-done((bf16[256,8192]{1,0:T(8,128)(2,1)S(1)}, bf16[256,8192]{1,0:T(8,128)(2,1)}, u32[]{:S(2)}) %copy-start) | copy-done | bytes 4194328
  3.6 0.0 copy-start.1
  3.6 0.9 %copy-done.1 = bf16[8,8192]{1,0:T(8,128)(2,1)S(1)} copy-done((bf16[8,8192]{1,0:T(8,128)(2,1)S(1)}, bf16[8,8192]{1,0:T(8,128)(2,1)}, u32[]{:S(2)}) %copy-start.1) | copy-done | bytes 131096
  4.5 0.0 copy-start.2
  4.5 0.8 %copy-done.2 = f32[8192]{0:T(1024)S(1)} copy-done((f32[8192]{0:T(1024)S(1)}, f32[8192]{0:T(1024)}, u32[]{:S(2)}) %copy-start.2) | copy-done | bytes 32792
  5.2 0.0 copy-start.3
  5.2 0.7 %copy-done.3 = s32[256]{0:T(256)S(1)} copy-done((s32[256]{0:T(256)S(1)}, s32[256]{0:T(256)}, u32[]{:S(2)}) %copy-start.3) | copy-done | bytes 1048
  5.9 33.0 %shard_map.68 = (bf16[512,128]{1,0:T(8,128)(2,1)S(1)}, bf16[256,128]{1,0:T(8,128)(2,1)S(1)}) custom-call(bf16[256,8192]{1,0:T(8,128)(2,1)S(1)} %copy-done, s32[1,256]{1,0:T(1,128)S(1)} %bitcast.3, s32[128,1]{1,0:T(8,128)S(1)} %copy.7.owner_ref, f32[1,8192]{1,0:T(1,128)S(1)} %bitcast.2, bf16[8,8192]{1,0:T(8,128)(2,1)S(1)} %copy-done.1), custom_call_target="tpu_custom_call" | custom-call | flops 536870912 | bytes 4194304 | tf_op jit(solution)/shard_map/pallas_call | solution.py:295
  38.9 0.7 %copy.10 = bf16[512,128]{1,0:T(8,128)(2,1)} copy(bf16[512,128]{1,0:T(8,128)(2,1)S(1)} %get-tuple-element.4) | data formatting | bytes 262144
  39.6 0.6 %copy.11 = bf16[256,128]{1,0:T(8,128)(2,1)} copy(bf16[256,128]{1,0:T(8,128)(2,1)S(1)} %get-tuple-element.5) | data formatting | bytes 131072
Async XLA Ops:
  1.4 2.2 %copy-start = (bf16[256,8192]{1,0:T(8,128)(2,1)S(1)}, bf16[256,8192]{1,0:T(8,128)(2,1)}, u32[]{:S(2)}) copy-start(bf16[256,8192]{1,0:T(8,128)(2,1)} %train_ref.1) | copy-start | bytes 12582916
  3.6 0.9 %copy-start.1 = (bf16[8,8192]{1,0:T(8,128)(2,1)S(1)}, bf16[8,8192]{1,0:T(8,128)(2,1)}, u32[]{:S(2)}) copy-start(bf16[8,8192]{1,0:T(8,128)(2,1)} %val_ref.1) | copy-start | bytes 393220
  4.5 0.8 %copy-start.2 = (f32[8192]{0:T(1024)S(1)}, f32[8192]{0:T(1024)}, u32[]{:S(2)}) copy-start(f32[8192]{0:T(1024)} %param.8) | copy-start | bytes 98308
  5.2 0.7 %copy-start.3 = (s32[256]{0:T(256)S(1)}, s32[256]{0:T(256)}, u32[]{:S(2)}) copy-start(s32[256]{0:T(256)} %param.6) | copy-start | bytes 3076

commit v3 on v2

--- a/solution.py
+++ b/solution.py
@@ -65,32 +65,34 @@
 STRIP = 16
 
 
-def hot_places(ids, owners, capacity):
-    pairs, rows = owners.shape[0], ids.shape[1]
+def hot_places(ids, owners, members, capacity):
+    pairs, rows = owners.shape[1], ids.shape[1]
     iota = lax.broadcasted_iota
-    owner_hot = (iota(jnp.int32, (pairs, 128), 1) == owners).astype(jnp.float32)
-    before = (iota(jnp.int32, (pairs, pairs), 1) < iota(jnp.int32, (pairs, pairs), 0)).astype(jnp.float32)
-    counts = jnp.dot(before.astype(jnp.bfloat16), owner_hot.astype(jnp.bfloat16), preferred_element_type=jnp.float32)
-    position = jnp.sum(counts * owner_hot, axis=1, keepdims=True)
-    place = owners.astype(jnp.float32) * capacity + position
-    pair_hot = (iota(jnp.int32, (pairs, rows), 0) == ids).astype(jnp.float32)
-    after = (iota(jnp.int32, (rows, rows), 0) < iota(jnp.int32, (rows, rows), 1)).astype(jnp.float32)
-    earlier = jnp.dot(pair_hot.astype(jnp.bfloat16), after.astype(jnp.bfloat16), preferred_element_type=jnp.float32)
-    slot = jnp.sum(pair_hot * place, axis=0, keepdims=True)
+    ones = lambda mask: mask.astype(jnp.float32)
+    narrow = lambda values: values.astype(jnp.bfloat16)
+    dot = functools.partial(jnp.dot, preferred_element_type=jnp.float32)
+    owner_hot = ones(iota(jnp.int32, (members, pairs), 0) == owners)
+    after = ones(iota(jnp.int32, (pairs, pairs), 0) < iota(jnp.int32, (pairs, pairs), 1))
+    counts = dot(narrow(owner_hot), narrow(after))
+    place = owners.astype(jnp.float32) * capacity + jnp.sum(counts * owner_hot, axis=0, keepdims=True)
+    pair_hot = ones(iota(jnp.int32, (pairs, rows), 0) == ids)
+    after = ones(iota(jnp.int32, (rows, rows), 0) < iota(jnp.int32, (rows, rows), 1))
+    earlier = dot(narrow(pair_hot), narrow(after))
+    slot = dot(narrow(jnp.broadcast_to(place, (16, pairs))), narrow(pair_hot))[:1]
     second = jnp.sum(pair_hot * earlier, axis=0, keepdims=True)
     return slot, second
 
 
 def kernel(
     members, capacity,
-    train_ref, ids_ref, owner_ref, moment_ref, val_ref,
+    train_ref, ids_hbm, owner_hbm, moment_hbm, val_hbm,
     influence_ref, gap_ref,
-    rows, pre, squares, held, hot, signed, outbox, inbox,
-    row_sem, z_send, x_send, y_send, c_send, held_sem, out_send, out_recv,
+    ids_ref, owner_ref, moment_ref, val_ref, rows, pre, squares, held, hot, signed, outbox, inbox,
+    row_sem, small_sem, z_send, x_send, y_send, d_send, c_send, held_sem, out_send, out_recv,
 ):
     depth = members // (2 * COLS)
     total, features = train_ref.shape
-    vals = val_ref.shape[0]
+    vals = val_hbm.shape[0]
     wide = features // CHUNKS
     half = wide // 2
     slots = members * capacity
@@ -105,11 +107,17 @@
         x = lax.rem(col + dx, COLS)
         return (z * COLS + x) * 2 + lax.rem(core + dc, 2)
 
-    here = (group, me)
     aside = (group, at(0, 1))
     across = (1 - group, me)
+    corner = (1 - group, at(0, 1))
     sibling = (group, at(0, 0, 1))
 
+    smalls = []
+    pairs = ((val_hbm, val_ref), (moment_hbm, moment_ref), (ids_hbm, ids_ref), (owner_hbm, owner_ref))
+    for i, (source, target) in enumerate(pairs):
+        copy = pltpu.make_async_copy(source, target, small_sem.at[i])
+        copy.start()
+        smalls.append(copy)
     fetches = []
     for k in range(CHUNKS):
         lanes = pl.ds(k * wide, wide)
@@ -121,13 +129,15 @@
     for step in range(1, members):
         pl.semaphore_signal(barrier, 1, device_id=(group, lax.rem(me + step, members)), device_id_type=MESH)
     pl.semaphore_signal(barrier, 1, device_id=across, device_id_type=MESH)
-
+    pl.semaphore_signal(barrier, 1, device_id=corner, device_id_type=MESH)
+
+    smalls[0].wait()
     val = val_ref[...].astype(jnp.float32)
     unit = val * lax.rsqrt(jnp.mean(val * val, axis=1, keepdims=True) + epsilon)
     for k in range(CHUNKS):
         both = [unit[:, k * wide + h * half : k * wide + (h + 1) * half] for h in range(2)]
         held[k, pl.ds(me, 1)] = jnp.concatenate(both, axis=0).astype(jnp.bfloat16)[None]
-    pl.semaphore_wait(barrier, members)
+    pl.semaphore_wait(barrier, members + 1)
 
     sends = []
 
@@ -151,8 +161,11 @@
     def to_side(k, dz):
         send(k, at(dz, 0), x_send.at[k, dz], aside)
 
-    def to_group(k, dz, dx):
-        send(k, at(dz, dx), y_send.at[k, dx * depth + dz], across)
+    def to_group(k, dz):
+        send(k, at(dz, 0), y_send.at[k, dz], across)
+
+    def to_corner(k, dz):
+        send(k, at(dz, 0), d_send.at[k, dz], corner)
 
     steps = range(1, depth)
     own = [2 * j + group for j in range(CHUNKS // 2)]
@@ -162,34 +175,32 @@
         for dz in steps:
             send(own[j], me, z_send.at[j, dz - 1], (group, at(dz, 0)))
         to_side(own[j], 0)
-        if j % 2:
-            to_side(other[j], 0)
+        to_side(other[j], 0)
         to_core(own[j], 0, 0)
         to_core(other[j], 0, 0)
 
     def from_z(j):
         for dz in steps:
             arrived(own[j], at(dz, 0))
+            to_corner(own[j], dz)
             to_side(own[j], dz)
-            to_group(own[j], dz, 0)
+            to_group(own[j], dz)
             to_core(own[j], dz, 0)
 
-    def side_own(j):
+    def side(j):
+        arrived(other[j], at(0, 1))
+        to_core(other[j], 0, 1)
         for dz in range(depth):
             arrived(own[j], at(dz, 1))
-            if j % 2 == 0:
-                to_group(own[j], dz, 1)
             to_core(own[j], dz, 1)
 
-    def group_near(j):
+    def near(j):
         for dz in steps:
             arrived(other[j], at(dz, 0))
-            if j % 2:
-                to_side(other[j], dz)
             to_core(other[j], dz, 0)
 
     def far(j):
-        for dz in range(depth):
+        for dz in steps:
             arrived(other[j], at(dz, 1))
             to_core(other[j], dz, 1)
 
@@ -224,26 +235,29 @@
             result = term if result is None else result + term
         return result
 
+    smalls[1].wait()
     pre[...] = 1.0 / (jnp.sqrt(moment_ref[...]) + 1e-08)
     scale(0)
     from_z(0)
     scale(1)
-    side_own(0)
     from_z(1)
+    side(0)
+    near(0)
     scale(2)
-    group_near(1)
-    group_near(0)
+    far(0)
     scale(3)
-    side_own(1)
-    far(0)
-    slot, second = hot_places(ids_ref[...], owner_ref[...], capacity)
+    side(1)
+    near(1)
+    smalls[2].wait()
+    smalls[3].wait()
+    slot, second = hot_places(ids_ref[...], owner_ref[...], members, capacity)
     place = lax.broadcasted_iota(jnp.int32, (2 * slots, total), 0).astype(jnp.float32)
     hot[...] = (place == 2 * slot + second).astype(jnp.float32).astype(jnp.bfloat16)
     place = lax.broadcasted_iota(jnp.int32, (slots, total), 0).astype(jnp.float32)
     signed[...] = jnp.where(place == slot, 1 - 2 * second, 0.0).astype(jnp.bfloat16)
+    far(1)
     from_core(0)
     live = product(0) + product(1)
-    far(1)
     from_core(1)
     live = live + product(2) + product(3)
     live = live * (lax.rsqrt(squares[...] / features + epsilon) / math.sqrt(features))
@@ -298,9 +312,13 @@
             jax.ShapeDtypeStruct((2 * slots, width), jnp.bfloat16),
             jax.ShapeDtypeStruct((slots, width), jnp.bfloat16),
         ),
-        in_specs=[pl.BlockSpec(memory_space=pl.ANY), vmem, vmem, vmem, vmem],
+        in_specs=[pl.BlockSpec(memory_space=pltpu.HBM)] * 5,
         out_specs=(vmem, vmem),
         scratch_shapes=[
+            pltpu.VMEM((1, total), jnp.int32),
+            pltpu.VMEM((1, total // 2), jnp.int32),
+            pltpu.VMEM((1, features), jnp.float32),
+            pltpu.VMEM((vals, features), jnp.bfloat16),
             pltpu.VMEM((total, features), jnp.bfloat16),
             pltpu.VMEM((1, features), jnp.float32),
             pltpu.VMEM((total, 1), jnp.float32),
@@ -310,7 +328,9 @@
             pltpu.VMEM((members, 3 * capacity, width), jnp.bfloat16),
             pltpu.VMEM((members, 3 * capacity, width), jnp.bfloat16),
             dma((CHUNKS,)),
+            dma((4,)),
             dma((CHUNKS // 2, depth)),
+            dma((CHUNKS, depth)),
             dma((CHUNKS, depth)),
             dma((CHUNKS, COLS * depth)),
             dma((CHUNKS, COLS * depth)),
@@ -319,12 +339,12 @@
             dma((members,)),
         ],
         compiler_params=pltpu.CompilerParams(
-            collective_id=0, has_side_effects=True, vmem_limit_bytes=48 * 2**20
+            collective_id=0, has_side_effects=True, vmem_limit_bytes=64 * 2**20
         ),
         cost_estimate=pl.CostEstimate(
             flops=2 * total * features * width, bytes_accessed=2 * total * features, transcendentals=0
         ),
-    )(train_rows, pair_ids.reshape(1, total), pair_owner, second_moment.reshape(1, features), val_rows)
+    )(train_rows, pair_ids.reshape(1, total), pair_owner.reshape(1, total // 2), second_moment.reshape(1, features), val_rows)
 
 
 def solution(mesh):

time: 40.5 us -> 35.6 us (0.88)
  local copies, waits for them, and re-layouts: 6.57 us -> 3.04 us
  Pallas kernels: 33 us -> 31.8 us
    unnamed x11 -> x2, local copies, waits for them, and re-layouts: 6.57 us -> 3.04 us
    pallas_call x1, Pallas kernels: 33 us -> 31.8 us  [on_device(): pl.pallas_call(functools.partial(kernel, members, capacity), out_shape=(j...]
where the time goes in v3:
time: 35.6 us; the launch traced here: 35.4 us
  Pallas kernels  31.8 us (89%)
  local copies, waits for them, and re-layouts  3.04 us (9%)
  between operations  0.64 us (2%)
    pallas_call x1, Pallas kernels, on_device(): pl.pallas_call(functools.partial(kernel, members, capacity), out_shape=(j...  31.8 us
    unnamed x2, local copies, waits for them, and re-layouts  3.04 us

profile of v3, /device:TPU:0, one launch (start us, length us, event | category | flops | bytes accessed | tf_op | source)
XLA Modules:
  0.0 35.4 jit_solution(6086950815564527588)
XLA Ops:
  0.6 31.8 %shard_map.68 = (bf16[512,128]{1,0:T(8,128)(2,1)}, bf16[256,128]{1,0:T(8,128)(2,1)}) custom-call(bf16[256,8192]{1,0:T(8,128)(2,1)} %train_ref.1, s32[1,256]{1,0:T(1,128)} %bitcast.4, s32[1,128]{1,0:T(1,128)} %bitcast.5, f32[1,8192]{1,0:T(1,128)} %bitcast.3, bf16[8,8192]{1,0:T(8,128)(2,1)} %val_hbm.1), custom_call_target="tpu_custom_call" | custom-call | flops 536870912 | bytes 4194304 | tf_op jit(solution)/shard_map/pallas_call | solution.py:309
  32.4 1.6 %copy.9 = bf16[512,128]{1,0:T(8,128)(2,1)} copy(bf16[512,128]{1,0:T(8,128)(2,1)} %get-tuple-element.4) | data formatting | bytes 262144
  34.0 1.5 %copy.10 = bf16[256,128]{1,0:T(8,128)(2,1)} copy(bf16[256,128]{1,0:T(8,128)(2,1)} %get-tuple-element.5) | data formatting | bytes 131072

commit v4 on v3

--- a/solution.py
+++ b/solution.py
@@ -86,9 +86,9 @@
 def kernel(
     members, capacity,
     train_ref, ids_hbm, owner_hbm, moment_hbm, val_hbm,
-    influence_ref, gap_ref,
-    ids_ref, owner_ref, moment_ref, val_ref, rows, pre, squares, held, hot, signed, outbox, inbox,
-    row_sem, small_sem, z_send, x_send, y_send, d_send, c_send, held_sem, out_send, out_recv,
+    inbox,
+    ids_ref, owner_ref, moment_ref, val_ref, rows, pre, squares, held, hot, signed, outbox,
+    row_sem, small_sem, z_send, x_send, y_send, d_send, c_send, held_sem, core_sem, out_send, out_recv,
 ):
     depth = members // (2 * COLS)
     total, features = train_ref.shape
@@ -109,6 +109,10 @@
 
     aside = (group, at(0, 1))
     across = (1 - group, me)
+
+    def slab(dz, dx):
+        return (core * COLS + lax.rem(col + dx, COLS)) * depth + lax.rem(layer + dz, depth)
+
     corner = (1 - group, at(0, 1))
     sibling = (group, at(0, 0, 1))
 
@@ -136,7 +140,7 @@
     unit = val * lax.rsqrt(jnp.mean(val * val, axis=1, keepdims=True) + epsilon)
     for k in range(CHUNKS):
         both = [unit[:, k * wide + h * half : k * wide + (h + 1) * half] for h in range(2)]
-        held[k, pl.ds(me, 1)] = jnp.concatenate(both, axis=0).astype(jnp.bfloat16)[None]
+        held[k, pl.ds(slab(0, 0), 1)] = jnp.concatenate(both, axis=0).astype(jnp.bfloat16)[None]
     pl.semaphore_wait(barrier, members + 1)
 
     sends = []
@@ -155,17 +159,26 @@
             device_id=sibling, device_id_type=MESH,
         ).wait_recv()
 
-    def to_core(k, dz, dx):
-        send(k, at(dz, dx), c_send.at[k, dx * depth + dz], sibling)
+    def core_copy(k, which, x):
+        block = held.at[k, pl.ds((which * COLS + x) * depth, depth)]
+        return pltpu.make_async_remote_copy(
+            src_ref=block, dst_ref=block, send_sem=c_send.at[k, x], recv_sem=core_sem.at[k, x],
+            device_id=sibling, device_id_type=MESH,
+        )
+
+    def to_core(k, dx):
+        copy = core_copy(k, core, lax.rem(col + dx, COLS))
+        copy.start()
+        sends.append(copy)
 
     def to_side(k, dz):
-        send(k, at(dz, 0), x_send.at[k, dz], aside)
+        send(k, slab(dz, 0), x_send.at[k, dz], aside)
 
     def to_group(k, dz):
-        send(k, at(dz, 0), y_send.at[k, dz], across)
+        send(k, slab(dz, 0), y_send.at[k, dz], across)
 
     def to_corner(k, dz):
-        send(k, at(dz, 0), d_send.at[k, dz], corner)
+        send(k, slab(dz, 0), d_send.at[k, dz], corner)
 
     steps = range(1, depth)
     own = [2 * j + group for j in range(CHUNKS // 2)]
@@ -173,42 +186,38 @@
 
     for j in range(CHUNKS // 2):
         for dz in steps:
-            send(own[j], me, z_send.at[j, dz - 1], (group, at(dz, 0)))
+            send(own[j], slab(0, 0), z_send.at[j, dz - 1], (group, at(dz, 0)))
         to_side(own[j], 0)
         to_side(other[j], 0)
-        to_core(own[j], 0, 0)
-        to_core(other[j], 0, 0)
 
     def from_z(j):
         for dz in steps:
-            arrived(own[j], at(dz, 0))
+            arrived(own[j], slab(dz, 0))
             to_corner(own[j], dz)
             to_side(own[j], dz)
             to_group(own[j], dz)
-            to_core(own[j], dz, 0)
+        to_core(own[j], 0)
 
     def side(j):
-        arrived(other[j], at(0, 1))
-        to_core(other[j], 0, 1)
+        arrived(other[j], slab(0, 1))
         for dz in range(depth):
-            arrived(own[j], at(dz, 1))
-            to_core(own[j], dz, 1)
+            arrived(own[j], slab(dz, 1))
+        to_core(own[j], 1)
 
     def near(j):
         for dz in steps:
-            arrived(other[j], at(dz, 0))
-            to_core(other[j], dz, 0)
+            arrived(other[j], slab(dz, 0))
+        to_core(other[j], 0)
 
     def far(j):
         for dz in steps:
-            arrived(other[j], at(dz, 1))
-            to_core(other[j], dz, 1)
+            arrived(other[j], slab(dz, 1))
+        to_core(other[j], 1)
 
     def from_core(j):
         for k in (own[j], other[j]):
-            for dz in range(depth):
-                for dx in range(COLS):
-                    arrived(k, at(dz, dx, 1))
+            for x in range(COLS):
+                core_copy(k, 1 - core, x).wait_recv()
 
     def scale(k):
         fetches[k].wait()
@@ -226,7 +235,8 @@
         lax.fori_loop(0, total // STRIP, strip, 0)
 
     def product(k):
-        block = held[k].astype(jnp.float32)
+        order = [(m % 2 * COLS + m // 2 % COLS) * depth + m // (2 * COLS) for m in range(members)]
+        block = jnp.stack([held[k, i] for i in order]).astype(jnp.float32)
         result = None
         for h in range(2):
             piece = block[:, h * vals : (h + 1) * vals].reshape(members * vals, half).astype(jnp.bfloat16)
@@ -279,18 +289,15 @@
         copy.start()
         sends.append(copy)
 
-    def place_block(m, ref):
-        influence_ref[pl.ds(pl.multiple_of(m * 2 * capacity, 2 * capacity), 2 * capacity), :] = ref[m, : 2 * capacity]
-        gap_ref[pl.ds(pl.multiple_of(m * capacity, capacity), capacity), :] = ref[m, 2 * capacity :]
-
-    place_block(me, outbox)
+    kept = pltpu.make_async_copy(outbox.at[me], inbox.at[me], out_send.at[0])
+    kept.start()
     for step in range(1, members):
         m = lax.rem(me + members - step, members)
         pltpu.make_async_remote_copy(
             src_ref=outbox.at[m], dst_ref=inbox.at[m], send_sem=out_send.at[0], recv_sem=out_recv.at[m],
             device_id=sibling, device_id_type=MESH,
         ).wait_recv()
-        place_block(m, inbox)
+    kept.wait()
     for copy in sends:
         copy.wait_send()
 
@@ -304,16 +311,12 @@
         return plain(train_rows, pair_ids, pair_owner, second_moment, val_rows)
     slots, width, wide = members * capacity, members * vals, features // CHUNKS
     depth = members // (2 * COLS)
-    vmem = pl.BlockSpec(memory_space=pltpu.VMEM)
     dma = pltpu.SemaphoreType.DMA
-    return pl.pallas_call(
+    arrived = pl.pallas_call(
         functools.partial(kernel, members, capacity),
-        out_shape=(
-            jax.ShapeDtypeStruct((2 * slots, width), jnp.bfloat16),
-            jax.ShapeDtypeStruct((slots, width), jnp.bfloat16),
-        ),
+        out_shape=jax.ShapeDtypeStruct((members, 3 * capacity, width), jnp.bfloat16),
         in_specs=[pl.BlockSpec(memory_space=pltpu.HBM)] * 5,
-        out_specs=(vmem, vmem),
+        out_specs=pl.BlockSpec(memory_space=pltpu.HBM),
         scratch_shapes=[
             pltpu.VMEM((1, total), jnp.int32),
             pltpu.VMEM((1, total // 2), jnp.int32),
@@ -326,15 +329,15 @@
             pltpu.VMEM((2 * slots, total), jnp.bfloat16),
             pltpu.VMEM((slots, total), jnp.bfloat16),
             pltpu.VMEM((members, 3 * capacity, width), jnp.bfloat16),
-            pltpu.VMEM((members, 3 * capacity, width), jnp.bfloat16),
             dma((CHUNKS,)),
             dma((4,)),
             dma((CHUNKS // 2, depth)),
             dma((CHUNKS, depth)),
             dma((CHUNKS, depth)),
-            dma((CHUNKS, COLS * depth)),
-            dma((CHUNKS, COLS * depth)),
+            dma((CHUNKS, depth)),
+            dma((CHUNKS, COLS)),
             dma((CHUNKS, members)),
+            dma((CHUNKS, COLS)),
             dma((members,)),
             dma((members,)),
         ],
@@ -345,6 +348,10 @@
             flops=2 * total * features * width, bytes_accessed=2 * total * features, transcendentals=0
         ),
     )(train_rows, pair_ids.reshape(1, total), pair_owner.reshape(1, total // 2), second_moment.reshape(1, features), val_rows)
+    return (
+        arrived[:, : 2 * capacity].reshape(2 * slots, width),
+        arrived[:, 2 * capacity :].reshape(slots, width),
+    )
 
 
 def solution(mesh):

time: 35.6 us -> 34.7 us (0.975)
  Pallas kernels: 31.8 us -> 30.9 us
    slice x0 -> x2, local copies, waits for them, and re-layouts: none -> 3.05 us  [the longest x1 1.57 us: on_device(): arrived[:, :2 * capacity].reshape(2 * slots, width)]
    unnamed x2 -> x0, local copies, waits for them, and re-layouts: 3.04 us -> none
    pallas_call x1, Pallas kernels: 31.8 us -> 30.9 us  [on_device(): pl.pallas_call(functools.partial(kernel, members, capacity), out_shape=ja...]
where the time goes in v4:
time: 34.7 us; the launch traced here: 34.6 us
  Pallas kernels  30.9 us (89%)
  local copies, waits for them, and re-layouts  3.05 us (9%)
  between operations  0.64 us (2%)
    pallas_call x1, Pallas kernels, on_device(): pl.pallas_call(functools.partial(kernel, members, capacity), out_shape=ja...  30.9 us
    slice x1, local copies, waits for them, and re-layouts, on_device(): arrived[:, :2 * capacity].reshape(2 * slots, width)  1.57 us
    slice x1, local copies, waits for them, and re-layouts, on_device(): arrived[:, 2 * capacity:].reshape(slots, width)  1.48 us

profile of v4, /device:TPU:0, one launch (start us, length us, event | category | flops | bytes accessed | tf_op | source)
XLA Modules:
  0.0 34.6 jit_solution(12531504067449130287)
XLA Ops:
  0.6 30.9 %shard_map.68 = bf16[16,48,128]{2,1,0:T(8,128)(2,1)} custom-call(bf16[256,8192]{1,0:T(8,128)(2,1)} %train_ref.1, s32[1,256]{1,0:T(1,128)} %bitcast.8, s32[1,128]{1,0:T(1,128)} %bitcast.9, f32[1,8192]{1,0:T(1,128)} %bitcast.7, bf16[8,8192]{1,0:T(8,128)(2,1)} %val_hbm.1), custom_call_target="tpu_custom_call" | custom-call | flops 536870912 | bytes 4194304 | tf_op jit(solution)/shard_map/pallas_call | solution.py:315
  31.5 1.5 %slice.7 = bf16[16,16,128]{2,1,0:T(8,128)(2,1)} slice(bf16[16,48,128]{2,1,0:T(8,128)(2,1)} %shard_map.68), slice={[0:16], [32:48], [0:128]} | slice | bytes 131072 | tf_op jit(solution)/shard_map/slice | solution.py:353
  33.0 1.6 %slice.6 = bf16[16,32,128]{2,1,0:T(8,128)(2,1)} slice(bf16[16,48,128]{2,1,0:T(8,128)(2,1)} %shard_map.68), slice={[0:16], [0:32], [0:128]} | slice | bytes 262144 | tf_op jit(solution)/shard_map/slice | solution.py:352

commit v5 on v4

--- a/solution.py
+++ b/solution.py
@@ -247,6 +247,13 @@
 
     smalls[1].wait()
     pre[...] = 1.0 / (jnp.sqrt(moment_ref[...]) + 1e-08)
+    smalls[2].wait()
+    smalls[3].wait()
+    slot, second = hot_places(ids_ref[...], owner_ref[...], members, capacity)
+    place = lax.broadcasted_iota(jnp.int32, (2 * slots, total), 0).astype(jnp.float32)
+    hot[...] = (place == 2 * slot + second).astype(jnp.float32).astype(jnp.bfloat16)
+    place = lax.broadcasted_iota(jnp.int32, (slots, total), 0).astype(jnp.float32)
+    signed[...] = jnp.where(place == slot, 1 - 2 * second, 0.0).astype(jnp.bfloat16)
     scale(0)
     from_z(0)
     scale(1)
@@ -258,13 +265,6 @@
     scale(3)
     side(1)
     near(1)
-    smalls[2].wait()
-    smalls[3].wait()
-    slot, second = hot_places(ids_ref[...], owner_ref[...], members, capacity)
-    place = lax.broadcasted_iota(jnp.int32, (2 * slots, total), 0).astype(jnp.float32)
-    hot[...] = (place == 2 * slot + second).astype(jnp.float32).astype(jnp.bfloat16)
-    place = lax.broadcasted_iota(jnp.int32, (slots, total), 0).astype(jnp.float32)
-    signed[...] = jnp.where(place == slot, 1 - 2 * second, 0.0).astype(jnp.bfloat16)
     far(1)
     from_core(0)
     live = product(0) + product(1)

time: 34.7 us -> 34.9 us (level)
  no operation moved by 1% of the time
where the time goes in v5:
time: 34.9 us; the launch traced here: 34.7 us
  Pallas kernels  31 us (89%)
  local copies, waits for them, and re-layouts  3.05 us (9%)
  between operations  0.64 us (2%)
    pallas_call x1, Pallas kernels, on_device(): pl.pallas_call(functools.partial(kernel, members, capacity), out_shape=ja...  31 us
    slice x1, local copies, waits for them, and re-layouts, on_device(): arrived[:, :2 * capacity].reshape(2 * slots, width)  1.57 us
    slice x1, local copies, waits for them, and re-layouts, on_device(): arrived[:, 2 * capacity:].reshape(slots, width)  1.48 us

profile of v5, /device:TPU:0, one launch (start us, length us, event | category | flops | bytes accessed | tf_op | source)
XLA Modules:
  0.0 34.7 jit_solution(5643306073006458382)
XLA Ops:
  0.6 31.0 %shard_map.68 = bf16[16,48,128]{2,1,0:T(8,128)(2,1)} custom-call(bf16[256,8192]{1,0:T(8,128)(2,1)} %train_ref.1, s32[1,256]{1,0:T(1,128)} %bitcast.8, s32[1,128]{1,0:T(1,128)} %bitcast.9, f32[1,8192]{1,0:T(1,128)} %bitcast.7, bf16[8,8192]{1,0:T(8,128)(2,1)} %val_hbm.1), custom_call_target="tpu_custom_call" | custom-call | flops 536870912 | bytes 4194304 | tf_op jit(solution)/shard_map/pallas_call | solution.py:315
  31.7 1.5 %slice.7 = bf16[16,16,128]{2,1,0:T(8,128)(2,1)} slice(bf16[16,48,128]{2,1,0:T(8,128)(2,1)} %shard_map.68), slice={[0:16], [32:48], [0:128]} | slice | bytes 131072 | tf_op jit(solution)/shard_map/slice | solution.py:353
  33.1 1.6 %slice.6 = bf16[16,32,128]{2,1,0:T(8,128)(2,1)} slice(bf16[16,48,128]{2,1,0:T(8,128)(2,1)} %shard_map.68), slice={[0:16], [0:32], [0:128]} | slice | bytes 262144 | tf_op jit(solution)/shard_map/slice | solution.py:352
